TPU v7x, 256 devices: a whole 4x4x8 slice. The times are simulated.
256 devices in a mesh: seq: 64 (over z, y, core), head: 4 (over x).
Axes of the slice: x: 4, y: 4, z: 8, core: 2. Of those that a mesh axis runs over, the one named last changes fastest.
Arguments:
- queries: bfloat16 [65536, 1024], P('seq', 'head'), may hold values from -0.69921875 to 0.69921875
- key_vectors: bfloat16 [65536, 1024], P('seq', 'head'), may hold values from -0.69921875 to 0.69921875
- values: bfloat16 [65536, 1024], P('seq', 'head'), may hold values from -0.69921875 to 0.69921875
- out_grad: bfloat16 [65536, 1024], P('seq', 'head'), may hold values from -6 to 6
- level_coef: float32 [17, 65536], P(None, 'seq'), may hold values from 0.25 to 4
- saved_states: bfloat16 [64, 6, 8, 128, 128], P('seq', None, 'head'), may hold values from -0.079589844 to 0.079589844
Outputs:
- query_grad: bfloat16 [65536, 1024], P('seq', 'head')
- key_grad: bfloat16 [65536, 1024], P('seq', 'head')
- value_grad: bfloat16 [65536, 1024], P('seq', 'head')
- coef_grad: float32 [17, 65536], P(None, 'seq')
All inputs are finite; a program needn't handle non-finite values.
Results may differ from a plain program's by a relative error of at most 0.0053.
Values sent between devices are 32-bit elements; how exact they have to be, the bound alone decides.
A program may use at most 128 MiB of HBM per device.

v0:
```python
import jax
import jax.numpy as jnp
from jax import lax
from jax.experimental import pallas as pl
from jax.experimental.pallas import tpu as pltpu
from jax.sharding import PartitionSpec as P

MESH = pl.DeviceIdType.MESH
F32 = jnp.float32
BF16 = jnp.bfloat16
TOK = 1024
BLK = 128
NB = TOK // BLK
LOCAL = 11
CROSS = 6
DIAG = 8
FAR = (3, 4, 5)


def level_weight(level):
    return 1.0 if level == 0 else 2.0 ** (-(level - 1) / 2.0)


def dot(a, b):
    return jnp.dot(a, b, preferred_element_type=F32)


def dot_nt(a, b):
    return lax.dot_general(a, b, (((1,), (1,)), ((), ())), preferred_element_type=F32)


def kernel(
    q_ref, k_ref, v_ref, g_ref, lc_ref, st_ref,
    qo_ref, ko_ref, vo_ref, co_ref,
    q_t, k_t, g_t, masks, s_loc, g_loc, k_acc, v_acc,
    grads, core_in, pair_sum, l0_in, l1_in, l2_in, y_in, y_sum,
    z5_in, z4_in, z3_in, state, near, coef_all,
    core_ss, core_rs, l0_ss, l0_rs, l1_ss, l1_rs, l2_ss, l2_rs, y_ss, y_rs,
    z5_ss, z5_rs, z4_ss, z4_rs, z3_ss, z3_rs, st_ss, st_rs, nr_ss, nr_rs, x_ss, x_rs,
):
    shard = lax.axis_index("seq")
    hx = lax.axis_index("head")
    c = lax.rem(shard, 2)
    y = lax.rem(shard // 2, 4)
    z = shard // 8

    def at(cc, yy, zz):
        return ((zz * 4 + yy) * 2 + cc, hx)

    def bit(j):
        return lax.rem(shard // (1 << j), 2)

    other = 1 - c
    plane = [(cc, k) for cc in range(2) for k in range(4) if cc or k]

    def plane_dev(cc, k):
        return lax.rem(c + cc, 2), lax.rem(y + k, 4)

    barrier = pltpu.get_barrier_semaphore()
    for cc, k in plane:
        pc, py = plane_dev(cc, k)
        pl.semaphore_signal(barrier, inc=1, device_id=at(pc, py, z), device_id_type=MESH)
    for k in range(1, 8):
        pl.semaphore_signal(barrier, inc=1, device_id=at(c, y, lax.rem(z + k, 8)), device_id_type=MESH)
    for k in range(1, 4):
        pl.semaphore_signal(barrier, inc=1, device_id=(shard, lax.rem(hx + k, 4)), device_id_type=MESH)

    for h in range(2):
        hs = slice(h * BLK, (h + 1) * BLK)
        g_t[h] = g_ref[:, hs].T
        q_t[h] = q_ref[:, hs].T
        k_t[h] = k_ref[:, hs].T
    for j in reversed(range(CROSS)):
        w = level_weight(LOCAL + j)
        row = lc_ref[LOCAL + j : LOCAL + j + 1, :]
        for h in range(2):
            hs = slice(h * BLK, (h + 1) * BLK)
            scaled = (g_t[h].astype(F32) * row).astype(BF16)
            grads[j, h] = (w * dot(scaled, q_ref[:, hs])).reshape(4, 32, BLK)

    key_pos = lax.broadcasted_iota(jnp.int32, (BLK, BLK), 0)
    query_pos = lax.broadcasted_iota(jnp.int32, (BLK, BLK), 1)
    mixed = jnp.bitwise_xor(key_pos, query_pos)
    level = jnp.zeros((BLK, BLK), jnp.int32)
    for b in range(DIAG - 1):
        level = level + (mixed >= (1 << b)).astype(jnp.int32)
    for n in range(DIAG):
        hit = jnp.logical_and(level == n, key_pos <= query_pos)
        masks[n] = jnp.where(hit, level_weight(n), 0.0).astype(F32)

    for h in range(2):
        hs = slice(h * BLK, (h + 1) * BLK)
        for n in range(4):
            r = slice(n * 256, n * 256 + 128)
            s_loc[h, n] = dot(k_t[h, :, r], v_ref[r, hs]).astype(BF16)
        for n in range(2):
            r = slice(n * 512, n * 512 + 256)
            s_loc[h, 4 + n] = dot(k_t[h, :, r], v_ref[r, hs]).astype(BF16)
        s_loc[h, 6] = dot(k_t[h, :, 0:512], v_ref[0:512, hs]).astype(BF16)
    g_loc[...] = jnp.zeros_like(g_loc)

    bits = [bit(j).astype(F32) for j in range(CROSS)]

    def block(i, carry):
        ts = pl.ds(pl.multiple_of(i * BLK, BLK), BLK)
        slots = (i // 2, 4 + i // 4, 6)
        right = [lax.rem(i // (1 << n), 2).astype(F32) for n in range(3)]
        rows = [lc_ref[n : n + 1, ts] for n in range(DIAG)]
        coef = masks[0] * rows[0]
        for n in range(1, DIAG):
            coef = coef + masks[n] * rows[n]
        local = [lc_ref[DIAG + n : DIAG + n + 1, ts] * (right[n] * level_weight(DIAG + n)) for n in range(3)]
        cross = [lc_ref[LOCAL + j : LOCAL + j + 1, ts] * bits[j] for j in range(CROSS)]
        prods = None
        sums = [None] * (3 + CROSS)
        for h in range(2):
            hs = slice(h * BLK, (h + 1) * BLK)
            q_i, k_i, v_i, g_i = q_ref[ts, hs], k_ref[ts, hs], v_ref[ts, hs], g_ref[ts, hs]
            qt, kt, gt = q_t[h, :, ts], k_t[h, :, ts], g_t[h, :, ts]
            scores = dot(k_i, qt)
            grad_scores = dot(v_i, gt)
            prod = scores * grad_scores
            prods = prod if prods is None else prods + prod
            weights = (coef * scores).astype(BF16)
            grad_weights = (coef * grad_scores).astype(BF16)
            k_acc[ts, hs] = dot(grad_weights, q_i)
            v_acc[ts, hs] = dot(weights, g_i)
            acc = dot(kt, grad_weights)
            qf, gf = qt.astype(F32), gt.astype(F32)
            for n in range(3 + CROSS):
                s = s_loc[h, slots[n]] if n < 3 else st_ref[0, n - 3, h]
                projected = dot(s, gt)
                acc = acc + projected * (local[n] if n < 3 else cross[n - 3])
                part = jnp.sum(qf * projected, axis=0, keepdims=True)
                sums[n] = part if sums[n] is None else sums[n] + part
            for n in range(3):
                g_loc[h, slots[n]] += dot((gf * local[n]).astype(BF16), q_i)
            qo_ref[ts, hs] = acc.T.astype(BF16)
        for n in range(DIAG):
            coef_all[hx, n : n + 1, ts] = jnp.sum(masks[n] * prods, axis=0, keepdims=True)
        for n in range(3):
            coef_all[hx, DIAG + n : DIAG + n + 1, ts] = sums[n] * (right[n] * level_weight(DIAG + n))
        for j in range(CROSS):
            coef_all[hx, LOCAL + j : LOCAL + j + 1, ts] = sums[3 + j] * bits[j]
        return carry

    lax.fori_loop(0, NB, block, 0)

    pl.semaphore_wait(barrier, len(plane) + 7 + 3)

    sends = []

    def copy(src, dst, ss, rs, dev):
        return pltpu.make_async_remote_copy(
            src_ref=src, dst_ref=dst, send_sem=ss, recv_sem=rs, device_id=dev, device_id_type=MESH
        )

    def send(cond, *args):
        def go():
            copy(*args).start()

        def done():
            copy(*args).wait_send()

        if cond is None:
            go()
        else:
            pl.when(cond)(go)
        sends.append((cond, done))

    mate = at(other, y, z)
    for j in (5, 4, 3, 2, 1):
        send(bit(j) == 1, grads.at[j, other], core_in.at[j], core_ss.at[j], core_rs.at[j], mate)
    send(c == 1, grads.at[0], l0_in, l0_ss, l0_rs, mate)
    for k in range(1, 4):
        send(
            None, coef_all.at[hx], coef_all.at[hx], x_ss.at[k - 1], x_rs.at[k - 1],
            (shard, lax.rem(hx + k, 4)),
        )

    def y_send(n, k):
        py = lax.rem(y + k, 4)
        return (pair_sum.at[FAR[n], py], y_in.at[n, k - 1], y_ss.at[n, k - 1], y_rs.at[n, k - 1], at(c, py, z))

    for j in (5, 4, 3, 2, 1):
        on = bit(j) == 1

        @pl.when(on)
        def _():
            copy(grads.at[j, other], core_in.at[j], core_ss.at[j], core_rs.at[j], mate).wait_recv()
            pair_sum[j] = grads[j, c] + core_in[j]

        if j in FAR:
            for k in range(1, 4):
                send(on, *y_send(FAR.index(j), k))
        elif j == 2:
            for k in range(2):
                send(on, pair_sum.at[2], l2_in.at[y - 2], l2_ss.at[k], l2_rs.at[y - 2], at(c, k, z))
        else:
            send(on, pair_sum.at[1], l1_in, l1_ss, l1_rs, at(c, y - 1, z))

    z5 = lambda k: (y_sum.at[2], z5_in.at[z - 4], z5_ss.at[k], z5_rs.at[z - 4], at(c, y, k))
    z4 = lambda k: (
        y_sum.at[1], z4_in.at[lax.rem(z, 2)], z4_ss.at[k], z4_rs.at[lax.rem(z, 2)], at(c, y, (z // 4) * 4 + k)
    )
    for n in (2, 1, 0):
        on = bit(FAR[n]) == 1

        @pl.when(on)
        def _():
            total = pair_sum[FAR[n], y]
            for k in range(1, 4):
                copy(*y_send(n, k)).wait_recv()
                total = total + y_in[n, k - 1]
            y_sum[n] = total

        if n == 2:
            for k in range(4):
                send(on, *z5(k))
        elif n == 1:
            for k in range(2):
                send(on, *z4(k))
        else:
            send(on, y_sum.at[0], z3_in, z3_ss, z3_rs, at(c, y, z - 1))

    near[c] = jnp.zeros((4, 32, BLK), F32)

    @pl.when(bit(2) == 0)
    def _():
        for k in range(2):
            copy(pair_sum.at[2], l2_in.at[k], l2_ss.at[k], l2_rs.at[k], at(c, y, z)).wait_recv()
        near[c] += l2_in[0] + l2_in[1]

    @pl.when(bit(1) == 0)
    def _():
        copy(pair_sum.at[1], l1_in, l1_ss, l1_rs, at(c, y, z)).wait_recv()
        near[c] += l1_in[...]

    send(None, near.at[c], near.at[c], nr_ss, nr_rs, mate)

    for k in range(1, 4):
        px = lax.rem(hx + 4 - k, 4)
        copy(
            coef_all.at[px], coef_all.at[px], x_ss.at[k - 1], x_rs.at[k - 1], (shard, px)
        ).wait_recv()
    co_ref[...] = ((coef_all[0] + coef_all[1]) + (coef_all[2] + coef_all[3]))

    some = z < 7

    @pl.when(z == 7)
    def _():
        state[...] = jnp.zeros_like(state)

    @pl.when(some)
    def _():
        state[c, y] = jnp.zeros((32, BLK), F32)

    @pl.when(bit(3) == 0)
    def _():
        copy(y_sum.at[0], z3_in, z3_ss, z3_rs, at(c, y, z)).wait_recv()
        state[c, y] += z3_in[...]

    @pl.when(bit(4) == 0)
    def _():
        for k in range(2):
            copy(y_sum.at[1], z4_in.at[k], z4_ss.at[k], z4_rs.at[k], at(c, y, z)).wait_recv()
        state[c, y] += z4_in[0] + z4_in[1]

    @pl.when(bit(5) == 0)
    def _():
        for k in range(4):
            copy(y_sum.at[2], z5_in.at[k], z5_ss.at[k], z5_rs.at[k], at(c, y, z)).wait_recv()
        state[c, y] += (z5_in[0] + z5_in[1]) + (z5_in[2] + z5_in[3])

    for n, (cc, k) in enumerate(plane):
        pc, py = plane_dev(cc, k)
        send(some, state.at[c, y], state.at[c, y], st_ss.at[n], st_rs.at[n], at(pc, py, z))

    copy(near.at[other], near.at[other], nr_ss, nr_rs, mate).wait_recv()

    @pl.when(c == 0)
    def _():
        copy(grads.at[0], l0_in, l0_ss, l0_rs, mate).wait_recv()

    @pl.when(c == 1)
    def _():
        l0_in[...] = jnp.zeros_like(l0_in)

    @pl.when(some)
    def _():
        for n, (cc, k) in enumerate(plane):
            sc, sy = lax.rem(c + cc, 2), lax.rem(y + 4 - k, 4)
            copy(state.at[sc, sy], state.at[sc, sy], st_ss.at[n], st_rs.at[n], at(sc, sy, z)).wait_recv()

    for h in range(2):
        hs = slice(h * BLK, (h + 1) * BLK)
        base = (state[h] + (near[h] + l0_in[h])).reshape(BLK, BLK)
        for i in range(NB):
            ts = slice(i * BLK, (i + 1) * BLK)
            total = base
            for n, slot in enumerate((i // 2, 4 + i // 4, 6)):
                if (i >> n) % 2 == 0:
                    total = total + g_loc[h, slot]
            gs = total.astype(BF16)
            ko_ref[ts, hs] = (k_acc[ts, hs] + dot(v_ref[ts, hs], gs)).astype(BF16)
            vo_ref[ts, hs] = (v_acc[ts, hs] + dot_nt(k_ref[ts, hs], gs)).astype(BF16)

    for cond, done in sends:
        if cond is None:
            done()
        else:
            pl.when(cond)(done)


def shards(queries, key_vectors, values, out_grad, level_coef, saved_states):
    sem = pltpu.SemaphoreType.DMA
    quarter = (4, 32, BLK)
    vmem = pl.BlockSpec(memory_space=pltpu.VMEM)
    return tuple(
        pl.pallas_call(
            kernel,
            out_shape=[jax.ShapeDtypeStruct((TOK, 2 * BLK), BF16)] * 3
            + [jax.ShapeDtypeStruct((LOCAL + CROSS, TOK), F32)],
            in_specs=[vmem] * 6,
            out_specs=[vmem] * 4,
            scratch_shapes=[
                pltpu.VMEM((2, BLK, TOK), BF16),
                pltpu.VMEM((2, BLK, TOK), BF16),
                pltpu.VMEM((2, BLK, TOK), BF16),
                pltpu.VMEM((DIAG, BLK, BLK), F32),
                pltpu.VMEM((2, 7, BLK, BLK), BF16),
                pltpu.VMEM((2, 7, BLK, BLK), F32),
                pltpu.VMEM((TOK, 2 * BLK), F32),
                pltpu.VMEM((TOK, 2 * BLK), F32),
                pltpu.VMEM((CROSS, 2) + quarter, F32),
                pltpu.VMEM((CROSS,) + quarter, F32),
                pltpu.VMEM((CROSS,) + quarter, F32),
                pltpu.VMEM((2,) + quarter, F32),
                pltpu.VMEM(quarter, F32),
                pltpu.VMEM((2,) + quarter, F32),
                pltpu.VMEM((3, 3, 32, BLK), F32),
                pltpu.VMEM((3, 32, BLK), F32),
                pltpu.VMEM((4, 32, BLK), F32),
                pltpu.VMEM((2, 32, BLK), F32),
                pltpu.VMEM((32, BLK), F32),
                pltpu.VMEM((2,) + quarter, F32),
                pltpu.VMEM((2,) + quarter, F32),
                pltpu.VMEM((4, LOCAL + CROSS, TOK), F32),
                sem((CROSS,)), sem((CROSS,)),
                sem, sem,
                sem, sem,
                sem((2,)), sem((2,)),
                sem((3, 3)), sem((3, 3)),
                sem((4,)), sem((4,)),
                sem((2,)), sem((2,)),
                sem, sem,
                sem((7,)), sem((7,)),
                sem, sem,
                sem((3,)), sem((3,)),
            ],
            compiler_params=pltpu.CompilerParams(
                collective_id=0, has_side_effects=True, vmem_limit_bytes=40 * 2**20
            ),
        )(queries, key_vectors, values, out_grad, level_coef, saved_states)
    )


def solution(mesh):
    in_specs = (
        P("seq", "head"),
        P("seq", "head"),
        P("seq", "head"),
        P("seq", "head"),
        P(None, "seq"),
        P("seq", None, "head", None, None),
    )
    out_specs = (P("seq", "head"), P("seq", "head"), P("seq", "head"), P(None, "seq"))
    return jax.shard_map(shards, mesh=mesh, in_specs=in_specs, out_specs=out_specs, check_vma=False)
```

profile of v0, /device:TPU:1, one launch (start us, length us, event | category | flops | bytes accessed | tf_op | source)
XLA Modules:
  0.0 38.6 jit_solution(3619387330589168191)
XLA Ops:
  0.6 0.0 copy-start
  0.6 1.0 %copy-done = bf16[1024,256]{1,0:T(8,128)(2,1)S(1)} copy-done((bf16[1024,256]{1,0:T(8,128)(2,1)S(1)}, bf16[1024,256]{1,0:T(8,128)(2,1)}, u32[]{:S(2)}) %copy-start) | copy-done | bytes 524312
  1.7 0.0 copy-start.1
  1.7 1.0 %copy-done.1 = bf16[1024,256]{1,0:T(8,128)(2,1)S(1)} copy-done((bf16[1024,256]{1,0:T(8,128)(2,1)S(1)}, bf16[1024,256]{1,0:T(8,128)(2,1)}, u32[]{:S(2)}) %copy-start.1) | copy-done | bytes 524312
  2.7 0.0 copy-start.2
  2.7 1.0 %copy-done.2 = bf16[1024,256]{1,0:T(8,128)(2,1)S(1)} copy-done((bf16[1024,256]{1,0:T(8,128)(2,1)S(1)}, bf16[1024,256]{1,0:T(8,128)(2,1)}, u32[]{:S(2)}) %copy-start.2) | copy-done | bytes 524312
  3.8 0.0 copy-start.3
  3.8 1.0 %copy-done.3 = bf16[1024,256]{1,0:T(8,128)(2,1)S(1)} copy-done((bf16[1024,256]{1,0:T(8,128)(2,1)S(1)}, bf16[1024,256]{1,0:T(8,128)(2,1)}, u32[]{:S(2)}) %copy-start.3) | copy-done | bytes 524312
  4.8 0.0 copy-start.4
  4.8 1.0 %copy-done.4 = bf16[1,6,2,128,128]{4,3,2,1,0:T(8,128)(2,1)S(1)} copy-done((bf16[1,6,2,128,128]{4,3,2,1,0:T(8,128)(2,1)S(1)}, bf16[1,6,2,128,128]{4,3,2,1,0:T(8,128)(2,1)}, u32[]{:S(2)}) %copy-start.4) | copy-done | bytes 393240
  5.8 0.0 copy-start.5
  5.8 0.9 %copy-done.5 = f32[17,1024]{1,0:T(8,128)S(1)} copy-done((f32[17,1024]{1,0:T(8,128)S(1)}, f32[17,1024]{1,0:T(8,128)}, u32[]{:S(2)}) %copy-start.5) | copy-done | bytes 69656
  6.7 28.9 %shard_map.93 = (bf16[1024,256]{1,0:T(8,128)(2,1)S(1)}, bf16[1024,256]{1,0:T(8,128)(2,1)S(1)}, bf16[1024,256]{1,0:T(8,128)(2,1)S(1)}, f32[17,1024]{1,0:T(8,128)S(1)}) custom-call(bf16[1024,256]{1,0:T(8,128)(2,1)S(1)} %copy-done, bf16[1024,256]{1,0:T(8,128)(2,1)S(1)} %copy-done.1, bf16[1024,256]{1,0:T(8,128)(2,1)S(1)} %copy-done.2, ...), custom_call_target="tpu_custom_call" | custom-call | tf_op jit(solution)/shard_map/pallas_call | solution.py:320
  35.6 0.8 %copy.14 = bf16[1024,256]{1,0:T(8,128)(2,1)} copy(bf16[1024,256]{1,0:T(8,128)(2,1)S(1)} %get-tuple-element.8) | data formatting | bytes 1048576
  36.4 0.8 %copy.15 = bf16[1024,256]{1,0:T(8,128)(2,1)} copy(bf16[1024,256]{1,0:T(8,128)(2,1)S(1)} %get-tuple-element.9) | data formatting | bytes 1048576
  37.2 0.8 %copy.16 = bf16[1024,256]{1,0:T(8,128)(2,1)} copy(bf16[1024,256]{1,0:T(8,128)(2,1)S(1)} %get-tuple-element.10) | data formatting | bytes 1048576
  38.0 0.6 %copy.17 = f32[17,1024]{1,0:T(8,128)} copy(f32[17,1024]{1,0:T(8,128)S(1)} %get-tuple-element.11) | data formatting | bytes 139264
Async XLA Ops:
  0.6 1.0 %copy-start = (bf16[1024,256]{1,0:T(8,128)(2,1)S(1)}, bf16[1024,256]{1,0:T(8,128)(2,1)}, u32[]{:S(2)}) copy-start(bf16[1024,256]{1,0:T(8,128)(2,1)} %q_ref.1) | copy-start | bytes 1572868
  1.7 1.0 %copy-start.1 = (bf16[1024,256]{1,0:T(8,128)(2,1)S(1)}, bf16[1024,256]{1,0:T(8,128)(2,1)}, u32[]{:S(2)}) copy-start(bf16[1024,256]{1,0:T(8,128)(2,1)} %k_ref.1) | copy-start | bytes 1572868
  2.7 1.0 %copy-start.2 = (bf16[1024,256]{1,0:T(8,128)(2,1)S(1)}, bf16[1024,256]{1,0:T(8,128)(2,1)}, u32[]{:S(2)}) copy-start(bf16[1024,256]{1,0:T(8,128)(2,1)} %v_ref.1) | copy-start | bytes 1572868
  3.8 1.0 %copy-start.3 = (bf16[1024,256]{1,0:T(8,128)(2,1)S(1)}, bf16[1024,256]{1,0:T(8,128)(2,1)}, u32[]{:S(2)}) copy-start(bf16[1024,256]{1,0:T(8,128)(2,1)} %g_ref.1) | copy-start | bytes 1572868
  4.8 1.0 %copy-start.4 = (bf16[1,6,2,128,128]{4,3,2,1,0:T(8,128)(2,1)S(1)}, bf16[1,6,2,128,128]{4,3,2,1,0:T(8,128)(2,1)}, u32[]{:S(2)}) copy-start(bf16[1,6,2,128,128]{4,3,2,1,0:T(8,128)(2,1)} %st_ref.1) | copy-start | bytes 1179652
  5.8 0.9 %copy-start.5 = (f32[17,1024]{1,0:T(8,128)S(1)}, f32[17,1024]{1,0:T(8,128)}, u32[]{:S(2)}) copy-start(f32[17,1024]{1,0:T(8,128)} %lc_ref.1) | copy-start | bytes 208900
where the time goes:
time: 39 us; the launch traced here: 38.6 us
  Pallas kernels  28.9 us (74%)
  local copies, waits for them, and re-layouts  9.07 us (23%)
  between operations  0.66 us (2%)
    pallas_call x1, Pallas kernels, shards(): pl.pallas_call(kernel, out_shape=[jax.ShapeDtypeStruct((TOK, 2 * BLK), BF...  28.9 us
    unnamed x16, local copies, waits for them, and re-layouts  9.07 us

commit v1 on v0

--- a/solution.py
+++ b/solution.py
@@ -30,9 +30,10 @@
 
 
 def kernel(
-    q_ref, k_ref, v_ref, g_ref, lc_ref, st_ref,
-    qo_ref, ko_ref, vo_ref, co_ref,
-    q_t, k_t, g_t, masks, s_loc, g_loc, k_acc, v_acc,
+    q_hbm, k_hbm, v_hbm, g_hbm, lc_hbm, st_hbm,
+    qo_ref, k_ref, v_ref, k_acc, v_acc, gs_ref, co_ref,
+    q_ref, g_ref, lc_ref, st_ref, load_sem,
+    q_t, k_t, g_t, masks, s_loc, g_loc,
     grads, core_in, pair_sum, l0_in, l1_in, l2_in, y_in, y_sum,
     z5_in, z4_in, z3_in, state, near, coef_all,
     core_ss, core_rs, l0_ss, l0_rs, l1_ss, l1_rs, l2_ss, l2_rs, y_ss, y_rs,
@@ -56,6 +57,15 @@
     def plane_dev(cc, k):
         return lax.rem(c + cc, 2), lax.rem(y + k, 4)
 
+    loads = [
+        pltpu.make_async_copy(src, dst, load_sem.at[n])
+        for n, (src, dst) in enumerate(
+            ((g_hbm, g_ref), (lc_hbm, lc_ref), (q_hbm, q_ref), (k_hbm, k_ref), (v_hbm, v_ref), (st_hbm, st_ref))
+        )
+    ]
+    for load in loads:
+        load.start()
+
     barrier = pltpu.get_barrier_semaphore()
     for cc, k in plane:
         pc, py = plane_dev(cc, k)
@@ -65,11 +75,11 @@
     for k in range(1, 4):
         pl.semaphore_signal(barrier, inc=1, device_id=(shard, lax.rem(hx + k, 4)), device_id_type=MESH)
 
+    for n in range(3):
+        loads[n].wait()
     for h in range(2):
         hs = slice(h * BLK, (h + 1) * BLK)
         g_t[h] = g_ref[:, hs].T
-        q_t[h] = q_ref[:, hs].T
-        k_t[h] = k_ref[:, hs].T
     for j in reversed(range(CROSS)):
         w = level_weight(LOCAL + j)
         row = lc_ref[LOCAL + j : LOCAL + j + 1, :]
@@ -87,6 +97,13 @@
     for n in range(DIAG):
         hit = jnp.logical_and(level == n, key_pos <= query_pos)
         masks[n] = jnp.where(hit, level_weight(n), 0.0).astype(F32)
+
+    for n in range(3, 6):
+        loads[n].wait()
+    for h in range(2):
+        hs = slice(h * BLK, (h + 1) * BLK)
+        q_t[h] = q_ref[:, hs].T
+        k_t[h] = k_ref[:, hs].T
 
     for h in range(2):
         hs = slice(h * BLK, (h + 1) * BLK)
@@ -293,17 +310,13 @@
             copy(state.at[sc, sy], state.at[sc, sy], st_ss.at[n], st_rs.at[n], at(sc, sy, z)).wait_recv()
 
     for h in range(2):
-        hs = slice(h * BLK, (h + 1) * BLK)
         base = (state[h] + (near[h] + l0_in[h])).reshape(BLK, BLK)
         for i in range(NB):
-            ts = slice(i * BLK, (i + 1) * BLK)
             total = base
             for n, slot in enumerate((i // 2, 4 + i // 4, 6)):
                 if (i >> n) % 2 == 0:
                     total = total + g_loc[h, slot]
-            gs = total.astype(BF16)
-            ko_ref[ts, hs] = (k_acc[ts, hs] + dot(v_ref[ts, hs], gs)).astype(BF16)
-            vo_ref[ts, hs] = (v_acc[ts, hs] + dot_nt(k_ref[ts, hs], gs)).astype(BF16)
+            gs_ref[h, i] = total.astype(BF16)
 
     for cond, done in sends:
         if cond is None:
@@ -312,26 +325,57 @@
             pl.when(cond)(done)
 
 
+def finish(
+    qi_ref, k_ref, v_ref, k_acc, v_acc, gs_ref, ci_ref,
+    qo_hbm, ko_hbm, vo_hbm, co_hbm,
+    ko, vo, sem,
+):
+    writes = [
+        pltpu.make_async_copy(qi_ref, qo_hbm, sem.at[0]),
+        pltpu.make_async_copy(ci_ref, co_hbm, sem.at[1]),
+    ]
+    for write in writes:
+        write.start()
+    for i in range(NB):
+        ts = slice(i * BLK, (i + 1) * BLK)
+        for h in range(2):
+            hs = slice(h * BLK, (h + 1) * BLK)
+            gs = gs_ref[h, i]
+            ko[ts, hs] = (k_acc[ts, hs] + dot(v_ref[ts, hs], gs)).astype(BF16)
+            vo[ts, hs] = (v_acc[ts, hs] + dot_nt(k_ref[ts, hs], gs)).astype(BF16)
+        for n, (src, dst) in enumerate(((ko, ko_hbm), (vo, vo_hbm))):
+            write = pltpu.make_async_copy(src.at[ts], dst.at[ts], sem.at[2 + 2 * i + n])
+            write.start()
+            writes.append(write)
+    for write in writes:
+        write.wait()
+
+
 def shards(queries, key_vectors, values, out_grad, level_coef, saved_states):
     sem = pltpu.SemaphoreType.DMA
     quarter = (4, 32, BLK)
     vmem = pl.BlockSpec(memory_space=pltpu.VMEM)
-    return tuple(
-        pl.pallas_call(
+    hbm = pl.BlockSpec(memory_space=pltpu.HBM)
+    tokens = jax.ShapeDtypeStruct((TOK, 2 * BLK), BF16)
+    sums = jax.ShapeDtypeStruct((TOK, 2 * BLK), F32)
+    coefs = jax.ShapeDtypeStruct((LOCAL + CROSS, TOK), F32)
+    parts = pl.pallas_call(
             kernel,
-            out_shape=[jax.ShapeDtypeStruct((TOK, 2 * BLK), BF16)] * 3
-            + [jax.ShapeDtypeStruct((LOCAL + CROSS, TOK), F32)],
-            in_specs=[vmem] * 6,
-            out_specs=[vmem] * 4,
+            out_shape=[tokens] * 3 + [sums] * 2 + [jax.ShapeDtypeStruct((2, NB, BLK, BLK), BF16), coefs],
+            in_specs=[hbm] * 6,
+            out_specs=[vmem] * 7,
             scratch_shapes=[
+                pltpu.VMEM((TOK, 2 * BLK), BF16),
+                pltpu.VMEM((TOK, 2 * BLK), BF16),
+                pltpu.VMEM((LOCAL + CROSS, TOK), F32),
+                pltpu.VMEM((1, CROSS, 2, BLK, BLK), BF16),
+                sem((6,)),
                 pltpu.VMEM((2, BLK, TOK), BF16),
                 pltpu.VMEM((2, BLK, TOK), BF16),
                 pltpu.VMEM((2, BLK, TOK), BF16),
                 pltpu.VMEM((DIAG, BLK, BLK), F32),
                 pltpu.VMEM((2, 7, BLK, BLK), BF16),
                 pltpu.VMEM((2, 7, BLK, BLK), F32),
-                pltpu.VMEM((TOK, 2 * BLK), F32),
-                pltpu.VMEM((TOK, 2 * BLK), F32),
                 pltpu.VMEM((CROSS, 2) + quarter, F32),
                 pltpu.VMEM((CROSS,) + quarter, F32),
                 pltpu.VMEM((CROSS,) + quarter, F32),
@@ -361,7 +405,20 @@
             compiler_params=pltpu.CompilerParams(
                 collective_id=0, has_side_effects=True, vmem_limit_bytes=40 * 2**20
             ),
-        )(queries, key_vectors, values, out_grad, level_coef, saved_states)
+        )(*[pltpu.with_memory_space_constraint(a, pltpu.HBM) for a in (queries, key_vectors, values, out_grad, level_coef, saved_states)])
+    return tuple(
+        pl.pallas_call(
+            finish,
+            out_shape=[tokens] * 3 + [coefs],
+            in_specs=[vmem] * 7,
+            out_specs=[hbm] * 4,
+            scratch_shapes=[
+                pltpu.VMEM((TOK, 2 * BLK), BF16),
+                pltpu.VMEM((TOK, 2 * BLK), BF16),
+                sem((2 + 2 * NB,)),
+            ],
+            compiler_params=pltpu.CompilerParams(vmem_limit_bytes=16 * 2**20),
+        )(*parts)
     )
 
 

time: 39 us -> 32 us (0.82)
  local copies, waits for them, and re-layouts: 9.07 us -> 0 us
  Pallas kernels: 28.9 us -> 31.2 us
    unnamed x16 -> x0, local copies, waits for them, and re-layouts: 9.07 us -> none
    pallas_call x1 -> x2, Pallas kernels: 28.9 us -> 31.2 us  [the longest x1 29.7 us: shards(): pl.pallas_call(kernel, out_shape=[tokens] * 3 + [sums] * 2 + [jax.ShapeDt...]
where the time goes in v1:
time: 32 us; the launch traced here: 31.9 us
  Pallas kernels  31.2 us (98%)
  between operations  0.64 us (2%)
    pallas_call x1, Pallas kernels, shards(): pl.pallas_call(kernel, out_shape=[tokens] * 3 + [sums] * 2 + [jax.ShapeDt...  29.7 us
    pallas_call x1, Pallas kernels, shards(): pl.pallas_call(finish, out_shape=[tokens] * 3 + [coefs], in_specs=[vmem]...  1.5 us

profile of v1, /device:TPU:1, one launch (start us, length us, event | category | flops | bytes accessed | tf_op | source)
XLA Modules:
  0.0 31.9 jit_solution(6834933076656257595)
XLA Ops:
  0.6 29.7 %shard_map.93 = (bf16[1024,256]{1,0:T(8,128)(2,1)S(1)}, bf16[1024,256]{1,0:T(8,128)(2,1)S(1)}, bf16[1024,256]{1,0:T(8,128)(2,1)S(1)}, f32[1024,256]{1,0:T(8,128)...) custom-call(bf16[1024,256]{1,0:T(8,128)(2,1)} %q_hbm.1, ...), custom_call_target="tpu_custom_call" | custom-call | tf_op jit(solution)/shard_map/pallas_call | solution.py:362
  30.4 1.5 %shard_map.94 = (bf16[1024,256]{1,0:T(8,128)(2,1)}, bf16[1024,256]{1,0:T(8,128)(2,1)}, bf16[1024,256]{1,0:T(8,128)(2,1)}, f32[17,1024]{1,0:T(8,128)}) custom-call(bf16[1024,256]{1,0:T(8,128)(2,1)S(1)} %get-tuple-element.11.qi_ref, bf16[1024,256]{1,0:T(8,128)(2,1)S(1)} %get-tuple-element.12.k_ref, bf16[1024,256]{1,0:T(8,128)(2,1)S(1)} %get-tuple-element.13.v_ref, ...), custom_call_target="tpu_custom_call" | custom-call | tf_op jit(solution)/shard_map/pallas_call | solution.py:410

commit v2 on v1

--- a/solution.py
+++ b/solution.py
@@ -36,7 +36,7 @@
     q_t, k_t, g_t, masks, s_loc, g_loc,
     grads, core_in, pair_sum, l0_in, l1_in, l2_in, y_in, y_sum,
     z5_in, z4_in, z3_in, state, near, coef_all,
-    core_ss, core_rs, l0_ss, l0_rs, l1_ss, l1_rs, l2_ss, l2_rs, y_ss, y_rs,
+    relay_sem, core_ss, core_rs, l0_ss, l0_rs, l1_ss, l1_rs, l2_ss, l2_rs, y_ss, y_rs,
     z5_ss, z5_rs, z4_ss, z4_rs, z3_ss, z3_rs, st_ss, st_rs, nr_ss, nr_rs, x_ss, x_rs,
 ):
     shard = lax.axis_index("seq")
@@ -70,7 +70,7 @@
     for cc, k in plane:
         pc, py = plane_dev(cc, k)
         pl.semaphore_signal(barrier, inc=1, device_id=at(pc, py, z), device_id_type=MESH)
-    for k in range(1, 8):
+    for k in (1, 7):
         pl.semaphore_signal(barrier, inc=1, device_id=at(c, y, lax.rem(z + k, 8)), device_id_type=MESH)
     for k in range(1, 4):
         pl.semaphore_signal(barrier, inc=1, device_id=(shard, lax.rem(hx + k, 4)), device_id_type=MESH)
@@ -161,9 +161,20 @@
             coef_all[hx, LOCAL + j : LOCAL + j + 1, ts] = sums[3 + j] * bits[j]
         return carry
 
-    lax.fori_loop(0, NB, block, 0)
-
-    pl.semaphore_wait(barrier, len(plane) + 7 + 3)
+    pl.semaphore_wait(barrier, len(plane) + 2 + 3)
+
+    def relay(step):
+        far = 1 << step
+        for way, k in enumerate((far, 8 - far)):
+            pl.semaphore_signal(
+                relay_sem.at[step, way], inc=1, device_id=at(c, y, lax.rem(z + k, 8)), device_id_type=MESH
+            )
+
+    def relayed(step):
+        for way in range(2):
+            pl.semaphore_wait(relay_sem.at[step, way], 1)
+
+    relay(0)
 
     sends = []
 
@@ -189,11 +200,8 @@
     for j in (5, 4, 3, 2, 1):
         send(bit(j) == 1, grads.at[j, other], core_in.at[j], core_ss.at[j], core_rs.at[j], mate)
     send(c == 1, grads.at[0], l0_in, l0_ss, l0_rs, mate)
-    for k in range(1, 4):
-        send(
-            None, coef_all.at[hx], coef_all.at[hx], x_ss.at[k - 1], x_rs.at[k - 1],
-            (shard, lax.rem(hx + k, 4)),
-        )
+    relayed(0)
+    relay(1)
 
     def y_send(n, k):
         py = lax.rem(y + k, 4)
@@ -210,13 +218,11 @@
         if j in FAR:
             for k in range(1, 4):
                 send(on, *y_send(FAR.index(j), k))
-        elif j == 2:
-            for k in range(2):
-                send(on, pair_sum.at[2], l2_in.at[y - 2], l2_ss.at[k], l2_rs.at[y - 2], at(c, k, z))
-        else:
-            send(on, pair_sum.at[1], l1_in, l1_ss, l1_rs, at(c, y - 1, z))
+
+    lax.fori_loop(0, NB // 2, block, 0)
 
     z5 = lambda k: (y_sum.at[2], z5_in.at[z - 4], z5_ss.at[k], z5_rs.at[z - 4], at(c, y, k))
+    relayed(1)
     z4 = lambda k: (
         y_sum.at[1], z4_in.at[lax.rem(z, 2)], z4_ss.at[k], z4_rs.at[lax.rem(z, 2)], at(c, y, (z // 4) * 4 + k)
     )
@@ -240,6 +246,18 @@
         else:
             send(on, y_sum.at[0], z3_in, z3_ss, z3_rs, at(c, y, z - 1))
 
+    for k in range(2):
+        send(bit(2) == 1, pair_sum.at[2], l2_in.at[y - 2], l2_ss.at[k], l2_rs.at[y - 2], at(c, k, z))
+    send(bit(1) == 1, pair_sum.at[1], l1_in, l1_ss, l1_rs, at(c, y - 1, z))
+
+    lax.fori_loop(NB // 2, NB, block, 0)
+
+    for k in range(1, 4):
+        send(
+            None, coef_all.at[hx], coef_all.at[hx], x_ss.at[k - 1], x_rs.at[k - 1],
+            (shard, lax.rem(hx + k, 4)),
+        )
+
     near[c] = jnp.zeros((4, 32, BLK), F32)
 
     @pl.when(bit(2) == 0)
@@ -254,6 +272,37 @@
         near[c] += l1_in[...]
 
     send(None, near.at[c], near.at[c], nr_ss, nr_rs, mate)
+
+    some = z < 7
+
+    @pl.when(z == 7)
+    def _():
+        state[...] = jnp.zeros_like(state)
+
+    @pl.when(some)
+    def _():
+        state[c, y] = jnp.zeros((32, BLK), F32)
+
+    @pl.when(bit(3) == 0)
+    def _():
+        copy(y_sum.at[0], z3_in, z3_ss, z3_rs, at(c, y, z)).wait_recv()
+        state[c, y] += z3_in[...]
+
+    @pl.when(bit(4) == 0)
+    def _():
+        for k in range(2):
+            copy(y_sum.at[1], z4_in.at[k], z4_ss.at[k], z4_rs.at[k], at(c, y, z)).wait_recv()
+        state[c, y] += z4_in[0] + z4_in[1]
+
+    @pl.when(bit(5) == 0)
+    def _():
+        for k in range(4):
+            copy(y_sum.at[2], z5_in.at[k], z5_ss.at[k], z5_rs.at[k], at(c, y, z)).wait_recv()
+        state[c, y] += (z5_in[0] + z5_in[1]) + (z5_in[2] + z5_in[3])
+
+    for n, (cc, k) in enumerate(plane):
+        pc, py = plane_dev(cc, k)
+        send(some, state.at[c, y], state.at[c, y], st_ss.at[n], st_rs.at[n], at(pc, py, z))
 
     for k in range(1, 4):
         px = lax.rem(hx + 4 - k, 4)
@@ -261,37 +310,6 @@
             coef_all.at[px], coef_all.at[px], x_ss.at[k - 1], x_rs.at[k - 1], (shard, px)
         ).wait_recv()
     co_ref[...] = ((coef_all[0] + coef_all[1]) + (coef_all[2] + coef_all[3]))
-
-    some = z < 7
-
-    @pl.when(z == 7)
-    def _():
-        state[...] = jnp.zeros_like(state)
-
-    @pl.when(some)
-    def _():
-        state[c, y] = jnp.zeros((32, BLK), F32)
-
-    @pl.when(bit(3) == 0)
-    def _():
-        copy(y_sum.at[0], z3_in, z3_ss, z3_rs, at(c, y, z)).wait_recv()
-        state[c, y] += z3_in[...]
-
-    @pl.when(bit(4) == 0)
-    def _():
-        for k in range(2):
-            copy(y_sum.at[1], z4_in.at[k], z4_ss.at[k], z4_rs.at[k], at(c, y, z)).wait_recv()
-        state[c, y] += z4_in[0] + z4_in[1]
-
-    @pl.when(bit(5) == 0)
-    def _():
-        for k in range(4):
-            copy(y_sum.at[2], z5_in.at[k], z5_ss.at[k], z5_rs.at[k], at(c, y, z)).wait_recv()
-        state[c, y] += (z5_in[0] + z5_in[1]) + (z5_in[2] + z5_in[3])
-
-    for n, (cc, k) in enumerate(plane):
-        pc, py = plane_dev(cc, k)
-        send(some, state.at[c, y], state.at[c, y], st_ss.at[n], st_rs.at[n], at(pc, py, z))
 
     copy(near.at[other], near.at[other], nr_ss, nr_rs, mate).wait_recv()
 
@@ -390,6 +408,7 @@
                 pltpu.VMEM((2,) + quarter, F32),
                 pltpu.VMEM((2,) + quarter, F32),
                 pltpu.VMEM((4, LOCAL + CROSS, TOK), F32),
+                pltpu.SemaphoreType.REGULAR((2, 2)),
                 sem((CROSS,)), sem((CROSS,)),
                 sem, sem,
                 sem, sem,

time: 32 us -> 27.1 us (0.85)
  Pallas kernels: 31.2 us -> 26.4 us
    pallas_call x1, Pallas kernels: 29.7 us -> 24.9 us  [shards(): pl.pallas_call(kernel, out_shape=[tokens] * 3 + [sums] * 2 + [jax.ShapeDt...]
where the time goes in v2:
time: 27.1 us; the launch traced here: 27 us
  Pallas kernels  26.4 us (97%)
  between operations  0.64 us (2%)
    pallas_call x1, Pallas kernels, shards(): pl.pallas_call(kernel, out_shape=[tokens] * 3 + [sums] * 2 + [jax.ShapeDt...  24.9 us
    pallas_call x1, Pallas kernels, shards(): pl.pallas_call(finish, out_shape=[tokens] * 3 + [coefs], in_specs=[vmem]...  1.5 us

profile of v2, /device:TPU:1, one launch (start us, length us, event | category | flops | bytes accessed | tf_op | source)
XLA Modules:
  0.0 27.0 jit_solution(9980707723645212798)
XLA Ops:
  0.6 24.9 %shard_map.93 = (bf16[1024,256]{1,0:T(8,128)(2,1)S(1)}, bf16[1024,256]{1,0:T(8,128)(2,1)S(1)}, bf16[1024,256]{1,0:T(8,128)(2,1)S(1)}, f32[1024,256]{1,0:T(8,128)...) custom-call(bf16[1024,256]{1,0:T(8,128)(2,1)} %q_hbm.1, ...), custom_call_target="tpu_custom_call" | custom-call | tf_op jit(solution)/shard_map/pallas_call | solution.py:380
  25.5 1.5 %shard_map.94 = (bf16[1024,256]{1,0:T(8,128)(2,1)}, bf16[1024,256]{1,0:T(8,128)(2,1)}, bf16[1024,256]{1,0:T(8,128)(2,1)}, f32[17,1024]{1,0:T(8,128)}) custom-call(bf16[1024,256]{1,0:T(8,128)(2,1)S(1)} %get-tuple-element.11.qi_ref, bf16[1024,256]{1,0:T(8,128)(2,1)S(1)} %get-tuple-element.12.k_ref, bf16[1024,256]{1,0:T(8,128)(2,1)S(1)} %get-tuple-element.13.v_ref, ...), custom_call_target="tpu_custom_call" | custom-call | tf_op jit(solution)/shard_map/pallas_call | solution.py:429

commit v3 on v2

--- a/solution.py
+++ b/solution.py
@@ -33,7 +33,7 @@
     q_hbm, k_hbm, v_hbm, g_hbm, lc_hbm, st_hbm,
     qo_ref, k_ref, v_ref, k_acc, v_acc, gs_ref, co_ref,
     q_ref, g_ref, lc_ref, st_ref, load_sem,
-    q_t, k_t, g_t, masks, s_loc, g_loc,
+    q_t, k_t, g_t, masks, s_loc, g_loc, w_st, gw_st,
     grads, core_in, pair_sum, l0_in, l1_in, l2_in, y_in, y_sum,
     z5_in, z4_in, z3_in, state, near, coef_all,
     relay_sem, core_ss, core_rs, l0_ss, l0_rs, l1_ss, l1_rs, l2_ss, l2_rs, y_ss, y_rs,
@@ -57,12 +57,13 @@
     def plane_dev(cc, k):
         return lax.rem(c + cc, 2), lax.rem(y + k, 4)
 
-    loads = [
-        pltpu.make_async_copy(src, dst, load_sem.at[n])
-        for n, (src, dst) in enumerate(
-            ((g_hbm, g_ref), (lc_hbm, lc_ref), (q_hbm, q_ref), (k_hbm, k_ref), (v_hbm, v_ref), (st_hbm, st_ref))
-        )
-    ]
+    order = [pl.ds(pl.multiple_of(n * BLK, BLK), BLK) for n in (other, c)]
+    pairs = []
+    for hs in order:
+        pairs += [(g_hbm.at[:, hs], g_ref.at[:, hs]), (q_hbm.at[:, hs], q_ref.at[:, hs])]
+    pairs.insert(1, (lc_hbm, lc_ref))
+    pairs += [(k_hbm, k_ref), (v_hbm, v_ref), (st_hbm, st_ref)]
+    loads = [pltpu.make_async_copy(src, dst, load_sem.at[n]) for n, (src, dst) in enumerate(pairs)]
     for load in loads:
         load.start()
 
@@ -74,47 +75,6 @@
         pl.semaphore_signal(barrier, inc=1, device_id=at(c, y, lax.rem(z + k, 8)), device_id_type=MESH)
     for k in range(1, 4):
         pl.semaphore_signal(barrier, inc=1, device_id=(shard, lax.rem(hx + k, 4)), device_id_type=MESH)
-
-    for n in range(3):
-        loads[n].wait()
-    for h in range(2):
-        hs = slice(h * BLK, (h + 1) * BLK)
-        g_t[h] = g_ref[:, hs].T
-    for j in reversed(range(CROSS)):
-        w = level_weight(LOCAL + j)
-        row = lc_ref[LOCAL + j : LOCAL + j + 1, :]
-        for h in range(2):
-            hs = slice(h * BLK, (h + 1) * BLK)
-            scaled = (g_t[h].astype(F32) * row).astype(BF16)
-            grads[j, h] = (w * dot(scaled, q_ref[:, hs])).reshape(4, 32, BLK)
-
-    key_pos = lax.broadcasted_iota(jnp.int32, (BLK, BLK), 0)
-    query_pos = lax.broadcasted_iota(jnp.int32, (BLK, BLK), 1)
-    mixed = jnp.bitwise_xor(key_pos, query_pos)
-    level = jnp.zeros((BLK, BLK), jnp.int32)
-    for b in range(DIAG - 1):
-        level = level + (mixed >= (1 << b)).astype(jnp.int32)
-    for n in range(DIAG):
-        hit = jnp.logical_and(level == n, key_pos <= query_pos)
-        masks[n] = jnp.where(hit, level_weight(n), 0.0).astype(F32)
-
-    for n in range(3, 6):
-        loads[n].wait()
-    for h in range(2):
-        hs = slice(h * BLK, (h + 1) * BLK)
-        q_t[h] = q_ref[:, hs].T
-        k_t[h] = k_ref[:, hs].T
-
-    for h in range(2):
-        hs = slice(h * BLK, (h + 1) * BLK)
-        for n in range(4):
-            r = slice(n * 256, n * 256 + 128)
-            s_loc[h, n] = dot(k_t[h, :, r], v_ref[r, hs]).astype(BF16)
-        for n in range(2):
-            r = slice(n * 512, n * 512 + 256)
-            s_loc[h, 4 + n] = dot(k_t[h, :, r], v_ref[r, hs]).astype(BF16)
-        s_loc[h, 6] = dot(k_t[h, :, 0:512], v_ref[0:512, hs]).astype(BF16)
-    g_loc[...] = jnp.zeros_like(g_loc)
 
     bits = [bit(j).astype(F32) for j in range(CROSS)]
 
@@ -132,7 +92,7 @@
         sums = [None] * (3 + CROSS)
         for h in range(2):
             hs = slice(h * BLK, (h + 1) * BLK)
-            q_i, k_i, v_i, g_i = q_ref[ts, hs], k_ref[ts, hs], v_ref[ts, hs], g_ref[ts, hs]
+            k_i, v_i = k_ref[ts, hs], v_ref[ts, hs]
             qt, kt, gt = q_t[h, :, ts], k_t[h, :, ts], g_t[h, :, ts]
             scores = dot(k_i, qt)
             grad_scores = dot(v_i, gt)
@@ -140,18 +100,16 @@
             prods = prod if prods is None else prods + prod
             weights = (coef * scores).astype(BF16)
             grad_weights = (coef * grad_scores).astype(BF16)
-            k_acc[ts, hs] = dot(grad_weights, q_i)
-            v_acc[ts, hs] = dot(weights, g_i)
+            w_st[h, i] = weights
+            gw_st[h, i] = grad_weights
             acc = dot(kt, grad_weights)
-            qf, gf = qt.astype(F32), gt.astype(F32)
+            qf = qt.astype(F32)
             for n in range(3 + CROSS):
                 s = s_loc[h, slots[n]] if n < 3 else st_ref[0, n - 3, h]
                 projected = dot(s, gt)
                 acc = acc + projected * (local[n] if n < 3 else cross[n - 3])
                 part = jnp.sum(qf * projected, axis=0, keepdims=True)
                 sums[n] = part if sums[n] is None else sums[n] + part
-            for n in range(3):
-                g_loc[h, slots[n]] += dot((gf * local[n]).astype(BF16), q_i)
             qo_ref[ts, hs] = acc.T.astype(BF16)
         for n in range(DIAG):
             coef_all[hx, n : n + 1, ts] = jnp.sum(masks[n] * prods, axis=0, keepdims=True)
@@ -161,6 +119,42 @@
             coef_all[hx, LOCAL + j : LOCAL + j + 1, ts] = sums[3 + j] * bits[j]
         return carry
 
+    sends = []
+
+    def copy(src, dst, ss, rs, dev):
+        return pltpu.make_async_remote_copy(
+            src_ref=src, dst_ref=dst, send_sem=ss, recv_sem=rs, device_id=dev, device_id_type=MESH
+        )
+
+    def send(cond, *args):
+        def go():
+            copy(*args).start()
+
+        def done():
+            copy(*args).wait_send()
+
+        if cond is None:
+            go()
+        else:
+            pl.when(cond)(go)
+        sends.append((cond, done))
+
+    mate = at(other, y, z)
+
+    def state_grad(j, n, hs):
+        row = lc_ref[LOCAL + j : LOCAL + j + 1, :]
+        scaled = (g_t[n].astype(F32) * row).astype(BF16)
+        grads[j, n] = (level_weight(LOCAL + j) * dot(scaled, q_ref[:, hs])).reshape(4, 32, BLK)
+
+    def core_send(j):
+        send(bit(j) == 1, grads.at[j, other], core_in.at[j], core_ss.at[j], core_rs.at[j], mate)
+
+    loads[0].wait()
+    g_t[other] = g_ref[:, order[0]].T
+    loads[1].wait()
+    loads[2].wait()
+    for j in (5, 4, 3, 2, 1):
+        state_grad(j, other, order[0])
     pl.semaphore_wait(barrier, len(plane) + 2 + 3)
 
     def relay(step):
@@ -174,38 +168,22 @@
         for way in range(2):
             pl.semaphore_wait(relay_sem.at[step, way], 1)
 
+    for j in (5, 4, 3, 2, 1):
+        core_send(j)
     relay(0)
-
-    sends = []
-
-    def copy(src, dst, ss, rs, dev):
-        return pltpu.make_async_remote_copy(
-            src_ref=src, dst_ref=dst, send_sem=ss, recv_sem=rs, device_id=dev, device_id_type=MESH
-        )
-
-    def send(cond, *args):
-        def go():
-            copy(*args).start()
-
-        def done():
-            copy(*args).wait_send()
-
-        if cond is None:
-            go()
-        else:
-            pl.when(cond)(go)
-        sends.append((cond, done))
-
-    mate = at(other, y, z)
-    for j in (5, 4, 3, 2, 1):
-        send(bit(j) == 1, grads.at[j, other], core_in.at[j], core_ss.at[j], core_rs.at[j], mate)
-    send(c == 1, grads.at[0], l0_in, l0_ss, l0_rs, mate)
+    loads[3].wait()
+    g_t[c] = g_ref[:, order[1]].T
+    loads[4].wait()
+    for j in reversed(range(CROSS)):
+        state_grad(j, c, order[1])
+    state_grad(0, other, order[0])
     relayed(0)
     relay(1)
 
     def y_send(n, k):
         py = lax.rem(y + k, 4)
-        return (pair_sum.at[FAR[n], py], y_in.at[n, k - 1], y_ss.at[n, k - 1], y_rs.at[n, k - 1], at(c, py, z))
+        src = z3_in.at[py] if n == 0 else pair_sum.at[FAR[n], py]
+        return (src, y_in.at[n, k - 1], y_ss.at[n, k - 1], y_rs.at[n, k - 1], at(c, py, z))
 
     for j in (5, 4, 3, 2, 1):
         on = bit(j) == 1
@@ -215,18 +193,49 @@
             copy(grads.at[j, other], core_in.at[j], core_ss.at[j], core_rs.at[j], mate).wait_recv()
             pair_sum[j] = grads[j, c] + core_in[j]
 
-        if j in FAR:
+        if j >= 4:
             for k in range(1, 4):
                 send(on, *y_send(FAR.index(j), k))
-
-    lax.fori_loop(0, NB // 2, block, 0)
-
+        elif j == 3:
+            send(on, pair_sum.at[3], z3_in, z3_ss, z3_rs, at(c, y, z - 1))
+
+    send(c == 1, grads.at[0], l0_in, l0_ss, l0_rs, mate)
+
+    key_pos = lax.broadcasted_iota(jnp.int32, (BLK, BLK), 0)
+    query_pos = lax.broadcasted_iota(jnp.int32, (BLK, BLK), 1)
+    mixed = jnp.bitwise_xor(key_pos, query_pos)
+    level = jnp.zeros((BLK, BLK), jnp.int32)
+    for b in range(DIAG - 1):
+        level = level + (mixed >= (1 << b)).astype(jnp.int32)
+    for n in range(DIAG):
+        hit = jnp.logical_and(level == n, key_pos <= query_pos)
+        masks[n] = jnp.where(hit, level_weight(n), 0.0).astype(F32)
+
+    for n in range(5, 8):
+        loads[n].wait()
+    for h in range(2):
+        hs = slice(h * BLK, (h + 1) * BLK)
+        q_t[h] = q_ref[:, hs].T
+        k_t[h] = k_ref[:, hs].T
+
+    for h in range(2):
+        hs = slice(h * BLK, (h + 1) * BLK)
+        for n in range(4):
+            r = slice(n * 256, n * 256 + 128)
+            s_loc[h, n] = dot(k_t[h, :, r], v_ref[r, hs]).astype(BF16)
+        for n in range(2):
+            r = slice(n * 512, n * 512 + 256)
+            s_loc[h, 4 + n] = dot(k_t[h, :, r], v_ref[r, hs]).astype(BF16)
+        s_loc[h, 6] = dot(k_t[h, :, 0:512], v_ref[0:512, hs]).astype(BF16)
+
+    lax.fori_loop(0, 2, block, 0, unroll=2)
+
+    relayed(1)
     z5 = lambda k: (y_sum.at[2], z5_in.at[z - 4], z5_ss.at[k], z5_rs.at[z - 4], at(c, y, k))
-    relayed(1)
     z4 = lambda k: (
         y_sum.at[1], z4_in.at[lax.rem(z, 2)], z4_ss.at[k], z4_rs.at[lax.rem(z, 2)], at(c, y, (z // 4) * 4 + k)
     )
-    for n in (2, 1, 0):
+    for n in (2, 1):
         on = bit(FAR[n]) == 1
 
         @pl.when(on)
@@ -237,20 +246,23 @@
                 total = total + y_in[n, k - 1]
             y_sum[n] = total
 
-        if n == 2:
-            for k in range(4):
-                send(on, *z5(k))
-        elif n == 1:
-            for k in range(2):
-                send(on, *z4(k))
-        else:
-            send(on, y_sum.at[0], z3_in, z3_ss, z3_rs, at(c, y, z - 1))
+        for k in range(4 if n == 2 else 2):
+            send(on, *(z5(k) if n == 2 else z4(k)))
+
+    even = bit(3) == 0
+
+    @pl.when(even)
+    def _():
+        copy(pair_sum.at[3], z3_in, z3_ss, z3_rs, at(c, y, z)).wait_recv()
+
+    for k in range(1, 4):
+        send(even, *y_send(0, k))
 
     for k in range(2):
         send(bit(2) == 1, pair_sum.at[2], l2_in.at[y - 2], l2_ss.at[k], l2_rs.at[y - 2], at(c, k, z))
     send(bit(1) == 1, pair_sum.at[1], l1_in, l1_ss, l1_rs, at(c, y - 1, z))
 
-    lax.fori_loop(NB // 2, NB, block, 0)
+    lax.fori_loop(2, NB, block, 0, unroll=2)
 
     for k in range(1, 4):
         send(
@@ -283,10 +295,13 @@
     def _():
         state[c, y] = jnp.zeros((32, BLK), F32)
 
-    @pl.when(bit(3) == 0)
-    def _():
-        copy(y_sum.at[0], z3_in, z3_ss, z3_rs, at(c, y, z)).wait_recv()
-        state[c, y] += z3_in[...]
+    @pl.when(even)
+    def _():
+        total = z3_in[y]
+        for k in range(1, 4):
+            copy(*y_send(0, k)).wait_recv()
+            total = total + y_in[0, k - 1]
+        state[c, y] += total
 
     @pl.when(bit(4) == 0)
     def _():
@@ -303,6 +318,20 @@
     for n, (cc, k) in enumerate(plane):
         pc, py = plane_dev(cc, k)
         send(some, state.at[c, y], state.at[c, y], st_ss.at[n], st_rs.at[n], at(pc, py, z))
+
+    for h in range(2):
+        hs = slice(h * BLK, (h + 1) * BLK)
+        for n in range(7):
+            lev = 0 if n < 4 else 1 if n < 6 else 2
+            half = BLK << lev
+            start = (2 * (n - (0, 4, 6)[lev]) + 1) * half
+            r = slice(start, start + half)
+            row = lc_ref[DIAG + lev : DIAG + lev + 1, r] * level_weight(DIAG + lev)
+            g_loc[h, n] = dot((g_t[h, :, r].astype(F32) * row).astype(BF16), q_ref[r, hs])
+        for i in range(NB):
+            ts = slice(i * BLK, (i + 1) * BLK)
+            k_acc[ts, hs] = dot(gw_st[h, i], q_ref[ts, hs])
+            v_acc[ts, hs] = dot(w_st[h, i], g_ref[ts, hs])
 
     for k in range(1, 4):
         px = lax.rem(hx + 4 - k, 4)
@@ -387,13 +416,15 @@
                 pltpu.VMEM((TOK, 2 * BLK), BF16),
                 pltpu.VMEM((LOCAL + CROSS, TOK), F32),
                 pltpu.VMEM((1, CROSS, 2, BLK, BLK), BF16),
-                sem((6,)),
+                sem((8,)),
                 pltpu.VMEM((2, BLK, TOK), BF16),
                 pltpu.VMEM((2, BLK, TOK), BF16),
                 pltpu.VMEM((2, BLK, TOK), BF16),
                 pltpu.VMEM((DIAG, BLK, BLK), F32),
                 pltpu.VMEM((2, 7, BLK, BLK), BF16),
                 pltpu.VMEM((2, 7, BLK, BLK), F32),
+                pltpu.VMEM((2, NB, BLK, BLK), BF16),
+                pltpu.VMEM((2, NB, BLK, BLK), BF16),
                 pltpu.VMEM((CROSS, 2) + quarter, F32),
                 pltpu.VMEM((CROSS,) + quarter, F32),
                 pltpu.VMEM((CROSS,) + quarter, F32),
@@ -404,7 +435,7 @@
                 pltpu.VMEM((3, 32, BLK), F32),
                 pltpu.VMEM((4, 32, BLK), F32),
                 pltpu.VMEM((2, 32, BLK), F32),
-                pltpu.VMEM((32, BLK), F32),
+                pltpu.VMEM(quarter, F32),
                 pltpu.VMEM((2,) + quarter, F32),
                 pltpu.VMEM((2,) + quarter, F32),
                 pltpu.VMEM((4, LOCAL + CROSS, TOK), F32),

time: 27.1 us -> 26.1 us (0.963)
  Pallas kernels: 26.4 us -> 25.4 us
    pallas_call x1, Pallas kernels: 24.9 us -> 23.9 us  [shards(): pl.pallas_call(kernel, out_shape=[tokens] * 3 + [sums] * 2 + [jax.ShapeDt...]
where the time goes in v3:
time: 26.1 us; the launch traced here: 26 us
  Pallas kernels  25.4 us (97%)
  between operations  0.64 us (2%)
    pallas_call x1, Pallas kernels, shards(): pl.pallas_call(kernel, out_shape=[tokens] * 3 + [sums] * 2 + [jax.ShapeDt...  23.9 us
    pallas_call x1, Pallas kernels, shards(): pl.pallas_call(finish, out_shape=[tokens] * 3 + [coefs], in_specs=[vmem]...  1.5 us

profile of v3, /device:TPU:1, one launch (start us, length us, event | category | flops | bytes accessed | tf_op | source)
XLA Modules:
  0.0 26.0 jit_solution(18139390231742186803)
XLA Ops:
  0.6 23.9 %shard_map.93 = (bf16[1024,256]{1,0:T(8,128)(2,1)S(1)}, bf16[1024,256]{1,0:T(8,128)(2,1)S(1)}, bf16[1024,256]{1,0:T(8,128)(2,1)S(1)}, f32[1024,256]{1,0:T(8,128)...) custom-call(bf16[1024,256]{1,0:T(8,128)(2,1)} %q_hbm.1, ...), custom_call_target="tpu_custom_call" | custom-call | tf_op jit(solution)/shard_map/pallas_call | solution.py:409
  24.5 1.5 %shard_map.94 = (bf16[1024,256]{1,0:T(8,128)(2,1)}, bf16[1024,256]{1,0:T(8,128)(2,1)}, bf16[1024,256]{1,0:T(8,128)(2,1)}, f32[17,1024]{1,0:T(8,128)}) custom-call(bf16[1024,256]{1,0:T(8,128)(2,1)S(1)} %get-tuple-element.11.qi_ref, bf16[1024,256]{1,0:T(8,128)(2,1)S(1)} %get-tuple-element.12.k_ref, bf16[1024,256]{1,0:T(8,128)(2,1)S(1)} %get-tuple-element.13.v_ref, ...), custom_call_target="tpu_custom_call" | custom-call | tf_op jit(solution)/shard_map/pallas_call | solution.py:460

commit v4 on v3

--- a/solution.py
+++ b/solution.py
@@ -63,7 +63,9 @@
         pairs += [(g_hbm.at[:, hs], g_ref.at[:, hs]), (q_hbm.at[:, hs], q_ref.at[:, hs])]
     pairs.insert(1, (lc_hbm, lc_ref))
     pairs += [(k_hbm, k_ref), (v_hbm, v_ref), (st_hbm, st_ref)]
-    loads = [pltpu.make_async_copy(src, dst, load_sem.at[n]) for n, (src, dst) in enumerate(pairs)]
+    loads = [
+        pltpu.make_async_copy(src, dst, load_sem.at[(0, 1, 2, 3, 3, 4, 5, 6)[n]]) for n, (src, dst) in enumerate(pairs)
+    ]
     for load in loads:
         load.start()
 
@@ -130,14 +132,16 @@
         def go():
             copy(*args).start()
 
-        def done():
-            copy(*args).wait_send()
-
         if cond is None:
             go()
         else:
             pl.when(cond)(go)
-        sends.append((cond, done))
+
+    def sent(cond, ref, ss):
+        sends.append((cond, lambda: copy(ref, ref, ss, ss, mate).wait_send()))
+
+    def received(ref, rs):
+        copy(ref, ref, rs, rs, mate).wait_recv()
 
     mate = at(other, y, z)
 
@@ -147,7 +151,8 @@
         grads[j, n] = (level_weight(LOCAL + j) * dot(scaled, q_ref[:, hs])).reshape(4, 32, BLK)
 
     def core_send(j):
-        send(bit(j) == 1, grads.at[j, other], core_in.at[j], core_ss.at[j], core_rs.at[j], mate)
+        group = (2, 2, 2, 2, 1, 0)[j]
+        send(None, grads.at[j, other], core_in.at[j], core_ss, core_rs.at[group], mate)
 
     loads[0].wait()
     g_t[other] = g_ref[:, order[0]].T
@@ -159,21 +164,20 @@
 
     def relay(step):
         far = 1 << step
-        for way, k in enumerate((far, 8 - far)):
+        for k in (far, 8 - far):
             pl.semaphore_signal(
-                relay_sem.at[step, way], inc=1, device_id=at(c, y, lax.rem(z + k, 8)), device_id_type=MESH
+                relay_sem.at[step], inc=1, device_id=at(c, y, lax.rem(z + k, 8)), device_id_type=MESH
             )
 
     def relayed(step):
-        for way in range(2):
-            pl.semaphore_wait(relay_sem.at[step, way], 1)
+        pl.semaphore_wait(relay_sem.at[step], 2)
 
     for j in (5, 4, 3, 2, 1):
         core_send(j)
+    sent(None, core_in.at[pl.ds(1, 5)], core_ss)
     relay(0)
-    loads[3].wait()
+    pltpu.make_async_copy(g_ref, g_ref, load_sem.at[3]).wait()
     g_t[c] = g_ref[:, order[1]].T
-    loads[4].wait()
     for j in reversed(range(CROSS)):
         state_grad(j, c, order[1])
     state_grad(0, other, order[0])
@@ -183,23 +187,31 @@
     def y_send(n, k):
         py = lax.rem(y + k, 4)
         src = z3_in.at[py] if n == 0 else pair_sum.at[FAR[n], py]
-        return (src, y_in.at[n, k - 1], y_ss.at[n, k - 1], y_rs.at[n, k - 1], at(c, py, z))
+        return (src, y_in.at[n, k - 1], y_ss.at[n], y_rs.at[n], at(c, py, z))
 
     for j in (5, 4, 3, 2, 1):
         on = bit(j) == 1
 
-        @pl.when(on)
-        def _():
-            copy(grads.at[j, other], core_in.at[j], core_ss.at[j], core_rs.at[j], mate).wait_recv()
-            pair_sum[j] = grads[j, c] + core_in[j]
-
         if j >= 4:
-            for k in range(1, 4):
-                send(on, *y_send(FAR.index(j), k))
+            received(core_in.at[j], core_rs.at[5 - j])
+        elif j == 3:
+            received(core_in.at[pl.ds(1, 3)], core_rs.at[2])
+        pair_sum[j] = grads[j, c] + core_in[j]
+        if j >= 4:
+            n = FAR.index(j)
+
+            @pl.when(on)
+            def _():
+                for k in range(1, 4):
+                    copy(*y_send(n, k)).start()
+
+            sent(on, y_in.at[n], y_ss.at[n])
         elif j == 3:
             send(on, pair_sum.at[3], z3_in, z3_ss, z3_rs, at(c, y, z - 1))
+            sent(on, z3_in, z3_ss)
 
     send(c == 1, grads.at[0], l0_in, l0_ss, l0_rs, mate)
+    sent(c == 1, l0_in, l0_ss)
 
     key_pos = lax.broadcasted_iota(jnp.int32, (BLK, BLK), 0)
     query_pos = lax.broadcasted_iota(jnp.int32, (BLK, BLK), 1)
@@ -231,59 +243,64 @@
     lax.fori_loop(0, 2, block, 0, unroll=2)
 
     relayed(1)
-    z5 = lambda k: (y_sum.at[2], z5_in.at[z - 4], z5_ss.at[k], z5_rs.at[z - 4], at(c, y, k))
-    z4 = lambda k: (
-        y_sum.at[1], z4_in.at[lax.rem(z, 2)], z4_ss.at[k], z4_rs.at[lax.rem(z, 2)], at(c, y, (z // 4) * 4 + k)
-    )
-    for n in (2, 1):
+    def z5(k):
+        return (y_sum.at[2], z5_in.at[z - 4], z5_ss, z5_rs, at(c, y, lax.rem(z + k, 4)))
+
+    def z4(k):
+        slot = lax.rem(z, 2)
+        return (y_sum.at[1], z4_in.at[slot], z4_ss, z4_rs, at(c, y, (z // 4) * 4 + lax.rem(slot + k, 2)))
+
+    for n, dests, z_send, z_in, ss in ((2, (0, 1, 3, 2), z5, z5_in, z5_ss), (1, (0, 1), z4, z4_in, z4_ss)):
         on = bit(FAR[n]) == 1
 
         @pl.when(on)
         def _():
-            total = pair_sum[FAR[n], y]
-            for k in range(1, 4):
-                copy(*y_send(n, k)).wait_recv()
-                total = total + y_in[n, k - 1]
-            y_sum[n] = total
-
-        for k in range(4 if n == 2 else 2):
-            send(on, *(z5(k) if n == 2 else z4(k)))
+            received(y_in.at[n], y_rs.at[n])
+            y_sum[n] = pair_sum[FAR[n], y] + (y_in[n, 0] + (y_in[n, 1] + y_in[n, 2]))
+            for k in dests:
+                copy(*z_send(k)).start()
+
+        sent(on, z_in, ss)
 
     even = bit(3) == 0
 
     @pl.when(even)
     def _():
-        copy(pair_sum.at[3], z3_in, z3_ss, z3_rs, at(c, y, z)).wait_recv()
-
-    for k in range(1, 4):
-        send(even, *y_send(0, k))
+        received(z3_in, z3_rs)
+        for k in range(1, 4):
+            copy(*y_send(0, k)).start()
+
+    sent(even, y_in.at[0], y_ss.at[0])
 
     for k in range(2):
-        send(bit(2) == 1, pair_sum.at[2], l2_in.at[y - 2], l2_ss.at[k], l2_rs.at[y - 2], at(c, k, z))
+        send(bit(2) == 1, pair_sum.at[2], l2_in.at[y - 2], l2_ss, l2_rs, at(c, k, z))
+    sent(bit(2) == 1, l2_in, l2_ss)
     send(bit(1) == 1, pair_sum.at[1], l1_in, l1_ss, l1_rs, at(c, y - 1, z))
+    sent(bit(1) == 1, l1_in, l1_ss)
 
     lax.fori_loop(2, NB, block, 0, unroll=2)
 
     for k in range(1, 4):
         send(
-            None, coef_all.at[hx], coef_all.at[hx], x_ss.at[k - 1], x_rs.at[k - 1],
+            None, coef_all.at[hx], coef_all.at[hx], x_ss, x_rs,
             (shard, lax.rem(hx + k, 4)),
         )
+    sent(None, coef_all.at[pl.ds(0, 3)], x_ss)
 
     near[c] = jnp.zeros((4, 32, BLK), F32)
 
     @pl.when(bit(2) == 0)
     def _():
-        for k in range(2):
-            copy(pair_sum.at[2], l2_in.at[k], l2_ss.at[k], l2_rs.at[k], at(c, y, z)).wait_recv()
+        received(l2_in, l2_rs)
         near[c] += l2_in[0] + l2_in[1]
 
     @pl.when(bit(1) == 0)
     def _():
-        copy(pair_sum.at[1], l1_in, l1_ss, l1_rs, at(c, y, z)).wait_recv()
+        received(l1_in, l1_rs)
         near[c] += l1_in[...]
 
     send(None, near.at[c], near.at[c], nr_ss, nr_rs, mate)
+    sent(None, near.at[c], nr_ss)
 
     some = z < 7
 
@@ -291,33 +308,34 @@
     def _():
         state[...] = jnp.zeros_like(state)
 
+    own = c * 4 + y
+
     @pl.when(some)
     def _():
-        state[c, y] = jnp.zeros((32, BLK), F32)
+        state[own] = jnp.zeros((32, BLK), F32)
 
     @pl.when(even)
     def _():
-        total = z3_in[y]
-        for k in range(1, 4):
-            copy(*y_send(0, k)).wait_recv()
-            total = total + y_in[0, k - 1]
-        state[c, y] += total
+        received(y_in.at[0], y_rs.at[0])
+        state[own] += z3_in[y] + (y_in[0, 0] + (y_in[0, 1] + y_in[0, 2]))
 
     @pl.when(bit(4) == 0)
     def _():
-        for k in range(2):
-            copy(y_sum.at[1], z4_in.at[k], z4_ss.at[k], z4_rs.at[k], at(c, y, z)).wait_recv()
-        state[c, y] += z4_in[0] + z4_in[1]
+        received(z4_in, z4_rs)
+        state[own] += z4_in[0] + z4_in[1]
 
     @pl.when(bit(5) == 0)
     def _():
-        for k in range(4):
-            copy(y_sum.at[2], z5_in.at[k], z5_ss.at[k], z5_rs.at[k], at(c, y, z)).wait_recv()
-        state[c, y] += (z5_in[0] + z5_in[1]) + (z5_in[2] + z5_in[3])
-
-    for n, (cc, k) in enumerate(plane):
-        pc, py = plane_dev(cc, k)
-        send(some, state.at[c, y], state.at[c, y], st_ss.at[n], st_rs.at[n], at(pc, py, z))
+        received(z5_in, z5_rs)
+        state[own] += (z5_in[0] + z5_in[1]) + (z5_in[2] + z5_in[3])
+
+    @pl.when(some)
+    def _():
+        for cc, k in plane:
+            pc, py = plane_dev(cc, k)
+            copy(state.at[own], state.at[own], st_ss, st_rs, at(pc, py, z)).start()
+
+    sent(some, state.at[pl.ds(0, 7)], st_ss)
 
     for h in range(2):
         hs = slice(h * BLK, (h + 1) * BLK)
@@ -333,18 +351,14 @@
             k_acc[ts, hs] = dot(gw_st[h, i], q_ref[ts, hs])
             v_acc[ts, hs] = dot(w_st[h, i], g_ref[ts, hs])
 
-    for k in range(1, 4):
-        px = lax.rem(hx + 4 - k, 4)
-        copy(
-            coef_all.at[px], coef_all.at[px], x_ss.at[k - 1], x_rs.at[k - 1], (shard, px)
-        ).wait_recv()
+    received(coef_all.at[pl.ds(0, 3)], x_rs)
     co_ref[...] = ((coef_all[0] + coef_all[1]) + (coef_all[2] + coef_all[3]))
 
-    copy(near.at[other], near.at[other], nr_ss, nr_rs, mate).wait_recv()
+    received(near.at[other], nr_rs)
 
     @pl.when(c == 0)
     def _():
-        copy(grads.at[0], l0_in, l0_ss, l0_rs, mate).wait_recv()
+        received(l0_in, l0_rs)
 
     @pl.when(c == 1)
     def _():
@@ -352,12 +366,10 @@
 
     @pl.when(some)
     def _():
-        for n, (cc, k) in enumerate(plane):
-            sc, sy = lax.rem(c + cc, 2), lax.rem(y + 4 - k, 4)
-            copy(state.at[sc, sy], state.at[sc, sy], st_ss.at[n], st_rs.at[n], at(sc, sy, z)).wait_recv()
+        received(state.at[pl.ds(0, 7)], st_rs)
 
     for h in range(2):
-        base = (state[h] + (near[h] + l0_in[h])).reshape(BLK, BLK)
+        base = (state[4 * h : 4 * h + 4] + (near[h] + l0_in[h])).reshape(BLK, BLK)
         for i in range(NB):
             total = base
             for n, slot in enumerate((i // 2, 4 + i // 4, 6)):
@@ -416,7 +428,7 @@
                 pltpu.VMEM((TOK, 2 * BLK), BF16),
                 pltpu.VMEM((LOCAL + CROSS, TOK), F32),
                 pltpu.VMEM((1, CROSS, 2, BLK, BLK), BF16),
-                sem((8,)),
+                sem((7,)),
                 pltpu.VMEM((2, BLK, TOK), BF16),
                 pltpu.VMEM((2, BLK, TOK), BF16),
                 pltpu.VMEM((2, BLK, TOK), BF16),
@@ -436,21 +448,21 @@
                 pltpu.VMEM((4, 32, BLK), F32),
                 pltpu.VMEM((2, 32, BLK), F32),
                 pltpu.VMEM(quarter, F32),
-                pltpu.VMEM((2,) + quarter, F32),
+                pltpu.VMEM((8, 32, BLK), F32),
                 pltpu.VMEM((2,) + quarter, F32),
                 pltpu.VMEM((4, LOCAL + CROSS, TOK), F32),
-                pltpu.SemaphoreType.REGULAR((2, 2)),
-                sem((CROSS,)), sem((CROSS,)),
-                sem, sem,
-                sem, sem,
-                sem((2,)), sem((2,)),
-                sem((3, 3)), sem((3, 3)),
-                sem((4,)), sem((4,)),
-                sem((2,)), sem((2,)),
-                sem, sem,
-                sem((7,)), sem((7,)),
+                pltpu.SemaphoreType.REGULAR((2,)),
+                sem, sem((3,)),
+                sem, sem,
+                sem, sem,
                 sem, sem,
                 sem((3,)), sem((3,)),
+                sem, sem,
+                sem, sem,
+                sem, sem,
+                sem, sem,
+                sem, sem,
+                sem, sem,
             ],
             compiler_params=pltpu.CompilerParams(
                 collective_id=0, has_side_effects=True, vmem_limit_bytes=40 * 2**20

time: 26.1 us -> 25.7 us (0.985)
  Pallas kernels: 25.4 us -> 25 us
    pallas_call x1, Pallas kernels: 23.9 us -> 23.5 us  [shards(): pl.pallas_call(kernel, out_shape=[tokens] * 3 + [sums] * 2 + [jax.ShapeDt...]
where the time goes in v4:
time: 25.7 us; the launch traced here: 25.6 us
  Pallas kernels  25 us (97%)
  between operations  0.64 us (2%)
    pallas_call x1, Pallas kernels, shards(): pl.pallas_call(kernel, out_shape=[tokens] * 3 + [sums] * 2 + [jax.ShapeDt...  23.5 us
    pallas_call x1, Pallas kernels, shards(): pl.pallas_call(finish, out_shape=[tokens] * 3 + [coefs], in_specs=[vmem]...  1.5 us

profile of v4, /device:TPU:1, one launch (start us, length us, event | category | flops | bytes accessed | tf_op | source)
XLA Modules:
  0.0 25.6 jit_solution(5878868588811476600)
XLA Ops:
  0.6 23.5 %shard_map.93 = (bf16[1024,256]{1,0:T(8,128)(2,1)S(1)}, bf16[1024,256]{1,0:T(8,128)(2,1)S(1)}, bf16[1024,256]{1,0:T(8,128)(2,1)S(1)}, f32[1024,256]{1,0:T(8,128)...) custom-call(bf16[1024,256]{1,0:T(8,128)(2,1)} %q_hbm.1, ...), custom_call_target="tpu_custom_call" | custom-call | tf_op jit(solution)/shard_map/pallas_call | solution.py:421
  24.1 1.5 %shard_map.94 = (bf16[1024,256]{1,0:T(8,128)(2,1)}, bf16[1024,256]{1,0:T(8,128)(2,1)}, bf16[1024,256]{1,0:T(8,128)(2,1)}, f32[17,1024]{1,0:T(8,128)}) custom-call(bf16[1024,256]{1,0:T(8,128)(2,1)S(1)} %get-tuple-element.11.qi_ref, bf16[1024,256]{1,0:T(8,128)(2,1)S(1)} %get-tuple-element.12.k_ref, bf16[1024,256]{1,0:T(8,128)(2,1)S(1)} %get-tuple-element.13.v_ref, ...), custom_call_target="tpu_custom_call" | custom-call | tf_op jit(solution)/shard_map/pallas_call | solution.py:472

commit v5 on v4

--- a/solution.py
+++ b/solution.py
@@ -34,9 +34,9 @@
     qo_ref, k_ref, v_ref, k_acc, v_acc, gs_ref, co_ref,
     q_ref, g_ref, lc_ref, st_ref, load_sem,
     q_t, k_t, g_t, masks, s_loc, g_loc, w_st, gw_st,
-    grads, core_in, pair_sum, l0_in, l1_in, l2_in, y_in, y_sum,
+    grads, core_in, pair_sum, l0_in, l1_in, l2_in, p_in, y_in, y_sum,
     z5_in, z4_in, z3_in, state, near, coef_all,
-    relay_sem, core_ss, core_rs, l0_ss, l0_rs, l1_ss, l1_rs, l2_ss, l2_rs, y_ss, y_rs,
+    relay_sem, core_ss, core_rs, l0_ss, l0_rs, l1_ss, l1_rs, l2_ss, l2_rs, p_ss, p_rs, y_ss, y_rs,
     z5_ss, z5_rs, z4_ss, z4_rs, z3_ss, z3_rs, st_ss, st_rs, nr_ss, nr_rs, x_ss, x_rs,
 ):
     shard = lax.axis_index("seq")
@@ -151,15 +151,17 @@
         grads[j, n] = (level_weight(LOCAL + j) * dot(scaled, q_ref[:, hs])).reshape(4, 32, BLK)
 
     def core_send(j):
-        group = (2, 2, 2, 2, 1, 0)[j]
-        send(None, grads.at[j, other], core_in.at[j], core_ss, core_rs.at[group], mate)
+        send(None, grads.at[j, other], core_in.at[j], core_ss, core_rs, mate)
 
     loads[0].wait()
     g_t[other] = g_ref[:, order[0]].T
     loads[1].wait()
     loads[2].wait()
-    for j in (5, 4, 3, 2, 1):
-        state_grad(j, other, order[0])
+    pltpu.make_async_copy(g_ref, g_ref, load_sem.at[3]).wait()
+    g_t[c] = g_ref[:, order[1]].T
+    for j in (5, 4):
+        for n in range(2):
+            state_grad(j, (other, c)[n], order[n])
     pl.semaphore_wait(barrier, len(plane) + 2 + 3)
 
     def relay(step):
@@ -172,43 +174,38 @@
     def relayed(step):
         pl.semaphore_wait(relay_sem.at[step], 2)
 
-    for j in (5, 4, 3, 2, 1):
+    for j in (5, 4):
+        n = j - 4
+
+        @pl.when(bit(j) == 1)
+        def _():
+            for m, (cc, k) in enumerate(plane):
+                pc, py = plane_dev(cc, k)
+                copy(grads.at[j, pc, py], p_in.at[n, m], p_ss.at[n], p_rs.at[n], at(pc, py, z)).start()
+
+        sent(bit(j) == 1, p_in.at[n], p_ss.at[n])
+    relay(0)
+    for j in (3, 2, 1):
+        for n in range(2):
+            state_grad(j, (other, c)[n], order[n])
+    for j in (3, 2, 1):
         core_send(j)
-    sent(None, core_in.at[pl.ds(1, 5)], core_ss)
-    relay(0)
-    pltpu.make_async_copy(g_ref, g_ref, load_sem.at[3]).wait()
-    g_t[c] = g_ref[:, order[1]].T
-    for j in reversed(range(CROSS)):
-        state_grad(j, c, order[1])
+    sent(None, core_in.at[pl.ds(1, 3)], core_ss)
     state_grad(0, other, order[0])
+    state_grad(0, c, order[1])
     relayed(0)
     relay(1)
 
     def y_send(n, k):
         py = lax.rem(y + k, 4)
-        src = z3_in.at[py] if n == 0 else pair_sum.at[FAR[n], py]
+        src = z3_in.at[py]
         return (src, y_in.at[n, k - 1], y_ss.at[n], y_rs.at[n], at(c, py, z))
 
-    for j in (5, 4, 3, 2, 1):
-        on = bit(j) == 1
-
-        if j >= 4:
-            received(core_in.at[j], core_rs.at[5 - j])
-        elif j == 3:
-            received(core_in.at[pl.ds(1, 3)], core_rs.at[2])
+    received(core_in.at[pl.ds(1, 3)], core_rs)
+    for j in (3, 2, 1):
         pair_sum[j] = grads[j, c] + core_in[j]
-        if j >= 4:
-            n = FAR.index(j)
-
-            @pl.when(on)
-            def _():
-                for k in range(1, 4):
-                    copy(*y_send(n, k)).start()
-
-            sent(on, y_in.at[n], y_ss.at[n])
-        elif j == 3:
-            send(on, pair_sum.at[3], z3_in, z3_ss, z3_rs, at(c, y, z - 1))
-            sent(on, z3_in, z3_ss)
+    send(bit(3) == 1, pair_sum.at[3], z3_in, z3_ss, z3_rs, at(c, y, z - 1))
+    sent(bit(3) == 1, z3_in, z3_ss)
 
     send(c == 1, grads.at[0], l0_in, l0_ss, l0_rs, mate)
     sent(c == 1, l0_in, l0_ss)
@@ -255,8 +252,11 @@
 
         @pl.when(on)
         def _():
-            received(y_in.at[n], y_rs.at[n])
-            y_sum[n] = pair_sum[FAR[n], y] + (y_in[n, 0] + (y_in[n, 1] + y_in[n, 2]))
+            received(p_in.at[n - 1], p_rs.at[n - 1])
+            total = grads[FAR[n], c, y]
+            for m in range(7):
+                total = total + p_in[n - 1, m]
+            y_sum[n] = total
             for k in dests:
                 copy(*z_send(k)).start()
 
@@ -443,7 +443,8 @@
                 pltpu.VMEM((2,) + quarter, F32),
                 pltpu.VMEM(quarter, F32),
                 pltpu.VMEM((2,) + quarter, F32),
-                pltpu.VMEM((3, 3, 32, BLK), F32),
+                pltpu.VMEM((2, 7, 32, BLK), F32),
+                pltpu.VMEM((1, 3, 32, BLK), F32),
                 pltpu.VMEM((3, 32, BLK), F32),
                 pltpu.VMEM((4, 32, BLK), F32),
                 pltpu.VMEM((2, 32, BLK), F32),
@@ -452,11 +453,12 @@
                 pltpu.VMEM((2,) + quarter, F32),
                 pltpu.VMEM((4, LOCAL + CROSS, TOK), F32),
                 pltpu.SemaphoreType.REGULAR((2,)),
-                sem, sem((3,)),
-                sem, sem,
-                sem, sem,
-                sem, sem,
-                sem((3,)), sem((3,)),
+                sem, sem,
+                sem, sem,
+                sem, sem,
+                sem, sem,
+                sem((2,)), sem((2,)),
+                sem((1,)), sem((1,)),
                 sem, sem,
                 sem, sem,
                 sem, sem,

time: 25.7 us -> 25.5 us (level)
  Pallas kernels: 25 us -> 24.7 us
where the time goes in v5:
time: 25.5 us; the launch traced here: 25.4 us
  Pallas kernels  24.7 us (97%)
  between operations  0.64 us (3%)
    pallas_call x1, Pallas kernels, shards(): pl.pallas_call(kernel, out_shape=[tokens] * 3 + [sums] * 2 + [jax.ShapeDt...  23.2 us
    pallas_call x1, Pallas kernels, shards(): pl.pallas_call(finish, out_shape=[tokens] * 3 + [coefs], in_specs=[vmem]...  1.5 us

profile of v5, /device:TPU:1, one launch (start us, length us, event | category | flops | bytes accessed | tf_op | source)
XLA Modules:
  0.0 25.4 jit_solution(11131512111678399361)
XLA Ops:
  0.6 23.2 %shard_map.93 = (bf16[1024,256]{1,0:T(8,128)(2,1)S(1)}, bf16[1024,256]{1,0:T(8,128)(2,1)S(1)}, bf16[1024,256]{1,0:T(8,128)(2,1)S(1)}, f32[1024,256]{1,0:T(8,128)...) custom-call(bf16[1024,256]{1,0:T(8,128)(2,1)} %q_hbm.1, ...), custom_call_target="tpu_custom_call" | custom-call | tf_op jit(solution)/shard_map/pallas_call | solution.py:421
  23.9 1.5 %shard_map.94 = (bf16[1024,256]{1,0:T(8,128)(2,1)}, bf16[1024,256]{1,0:T(8,128)(2,1)}, bf16[1024,256]{1,0:T(8,128)(2,1)}, f32[17,1024]{1,0:T(8,128)}) custom-call(bf16[1024,256]{1,0:T(8,128)(2,1)S(1)} %get-tuple-element.11.qi_ref, bf16[1024,256]{1,0:T(8,128)(2,1)S(1)} %get-tuple-element.12.k_ref, bf16[1024,256]{1,0:T(8,128)(2,1)S(1)} %get-tuple-element.13.v_ref, ...), custom_call_target="tpu_custom_call" | custom-call | tf_op jit(solution)/shard_map/pallas_call | solution.py:474
